TPU v7x, 128 devices: a whole 4x4x4 slice. The times are simulated.
128 devices in a mesh: tm: 8 (over z, y_hi), feat: 16 (over y_lo, x, core).
Axes of the slice: x: 4, y: 4 (y_hi: 2, y_lo: 2; y = y_hi * 2 + y_lo), z: 4, core: 2. Of those that a mesh axis runs over, the one named last changes fastest.
Arguments:
- trajectory: float32 [32768, 2048], P('tm', 'feat'), may hold values from -8 to 9
Outputs:
- moments: float32 [4, 2048, 2048], P(None, 'feat', 'tm')
All inputs are finite; a program needn't handle non-finite values.
Results may differ from a plain program's by a relative error of at most 0.00035.
Values may be sent and summed in bfloat16 or wider, within the bound.
A program may use at most 128 MiB of HBM per device.

v0:
```python
import jax
import jax.numpy as jnp
from jax import lax
from jax.sharding import Mesh
from jax.sharding import PartitionSpec as P

HALO = 16
TM = ("tm_0", "tm_1")
lag_values = (0, 1, 4, 16)


def copy_for_each(array, axis):
    length = lax.axis_size(axis)
    return lax.all_to_all(
        jnp.broadcast_to(array[None], (length, *array.shape)), axis, 0, 0, tiled=True
    )


def over_copies(array, axis):
    return copy_for_each(array, axis).sum(axis=0)


def passed_along(value, axis, steps):
    count = lax.axis_size(axis)
    initial, last = (max(0, -steps), min(count, count - steps))
    return lax.ppermute(value, axis, [(source, source + steps) for source in range(initial, last)])


def summed_rows(array, axes, dim):
    for axis in axes:
        array = lax.psum_scatter(array, axis, scatter_dimension=dim, tiled=True)
    return array


def shards(trajectory):
    rows = trajectory.shape[0]
    frames = rows * lax.axis_size(TM)
    total = over_copies(jnp.sum(trajectory, axis=0), TM)
    mean = total / frames
    centered = (trajectory - mean).astype(jnp.bfloat16)
    gathered = lax.all_gather(centered, "feat", axis=1, tiled=True)
    tail = passed_along(gathered[:HALO], TM, -1)
    extended = jnp.concatenate([gathered, tail], axis=0)
    blocks = [
        lax.dot_general(
            centered,
            extended[lag : lag + rows],
            (((0,), (0,)), ((), ())),
            preferred_element_type=jnp.float32,
        )
        for lag in lag_values
    ]
    partial_sum = jnp.stack(blocks)
    summed = summed_rows(partial_sum, TM, 2)
    scales = jnp.sqrt(jnp.float32(frames) - jnp.array(lag_values, jnp.float32))
    return summed / scales[:, None, None]


def solution(mesh):
    torus = Mesh(mesh.devices.reshape(4, 2, mesh.shape["feat"]), ("tm_0", "tm_1", "feat"))
    in_specs = (P(TM, "feat"),)
    out_specs = P(None, "feat", TM)
    return jax.shard_map(
        shards, mesh=torus, in_specs=in_specs, out_specs=out_specs, check_vma=False
    )
```

profile of v0, /device:TPU:1, one launch (start us, length us, event | category | flops | bytes accessed | tf_op | source)
XLA Modules:
  0.0 244.3 jit_solution(2764542623991633967)
XLA Ops:
  6.5 0.0 all-gather.2.cloned.1.call-start
  6.5 2.1 reduce_sum.18
  8.7 14.8 %all_to_all.6 = f32[8,1,128]{2,1,0:T(1,128)S(1)} all-to-all(f32[8,1,128]{2,1,0:T(1,128)S(1)} %broadcast_in_dim.2), channel_id=1, replica_groups=mesh['tm_0'=4,'tm_1'=2,'feat'=16] {'tm_0','tm_1'}, dimensions={0} | all-to-all | bytes 8192 | tf_op jit(solution)/shard_map/all_to_all | solution.py:14
  23.5 2.7 %subtract_convert_fusion = bf16[4096,128]{1,0:T(8,128)(2,1)} fusion(f32[4096,128]{1,0:T(8,128)} %param.2, f32[128]{0:T(128)S(1)} %broadcast_multiply_fusion.1), kind=kLoop, calls=%fused_computation.11 | loop fusion | flops 1048576 | bytes 3146240 | tf_op jit(solution)/shard_map/convert_element_type | solution.py:40
  26.2 0.0 all-gather.2.cloned.1.call-update
  26.2 0.0 reduce-scatter.3.cloned.1.call-start
  26.3 98.0 %all-gather.2.cloned.1.call-done = bf16[4096,2048]{1,0:T(8,128)(2,1)} async-done(((bf16[4096,128]{1,0:T(8,128)(2,1)}), bf16[4096,2048]{1,0:T(8,128)(2,1)}) %all-gather.2.cloned.1.call-update) | async-done | bytes 16777232 | tf_op jit(solution)/shard_map/all_gather | solution.py:41
  124.3 0.0 slice-start
  124.3 1.6 slice.16
  125.9 0.0 slice-start.1
  125.9 1.5 collective-permute-start
  127.4 9.4 %constant_dynamic-update-slice_fusion.1 = bf16[4112,2048]{1,0:T(8,128)(2,1)S(1)} fusion(bf16[4096,2048]{1,0:T(8,128)(2,1)} %all-gather.2.cloned.1.call-done), kind=kLoop, calls=%fused_computation.14 | loop fusion | bytes 33554432
  136.8 0.0 slice-done
  136.8 0.0 slice-done.1
  136.8 0.0 slice-done.2
  136.8 0.0 slice-done.3
  136.9 4.6 %convolution_bitcast_fusion = f32[1,128,2048]{2,1,0:T(8,128)} fusion(bf16[4096,128]{1,0:T(8,128)(2,1)} %subtract_convert_fusion, bf16[4096,2048]{1,0:T(8,128)(2,1)S(1)} %bitcast.15), kind=kOutput, calls=%fused_computation.9 | convolution fusion | flops 2147483648 | bytes 18874368 | tf_op jit(solution)/shard_map/dot_general | solution.py:45
  141.5 0.0 collective-permute-done
  141.5 0.0 copy-start
  141.5 3.7 %fusion.9 = f32[1,128,2048]{2,1,0:T(8,128)S(1)} fusion(bf16[4096,128]{1,0:T(8,128)(2,1)} %subtract_convert_fusion, bf16[4112,2048]{1,0:T(8,128)(2,1)S(1)} %constant_dynamic-update-slice_fusion), kind=kOutput, calls=%fused_computation.8 | convolution fusion | flops 2147483648 | bytes 18874368 | tf_op jit(solution)/shard_map/dot_general | solution.py:45
  145.2 0.0 copy-done
  145.2 6.1 %fusion.12 = f32[1,128,2048]{2,1,0:T(8,128)} fusion(bf16[4096,128]{1,0:T(8,128)(2,1)S(1)} %copy-done, bf16[4112,2048]{1,0:T(8,128)(2,1)S(1)} %constant_dynamic-update-slice_fusion), kind=kOutput, calls=%fused_computation.10 | convolution fusion | flops 2147483648 | bytes 18874368 | tf_op jit(solution)/shard_map/dot_general | solution.py:45
  151.3 6.1 %fusion.6 = f32[1,128,2048]{2,1,0:T(8,128)} fusion(bf16[4096,128]{1,0:T(8,128)(2,1)S(1)} %copy-done, bf16[4112,2048]{1,0:T(8,128)(2,1)S(1)} %constant_dynamic-update-slice_fusion), kind=kOutput, calls=%fused_computation.7 | convolution fusion | flops 2147483648 | bytes 18874368 | tf_op jit(solution)/shard_map/dot_general | solution.py:45
  157.4 0.0 copy-done.1
  157.4 3.9 %pad_maximum_fusion = f32[4,128,2048]{2,1,0:T(8,128)} fusion(f32[1,128,2048]{2,1,0:T(8,128)S(1)} %fusion.9, f32[1,128,2048]{2,1,0:T(8,128)} %fusion.12, f32[1,128,2048]{2,1,0:T(8,128)} %fusion.6, f32[1,128,2048]{2,1,0:T(8,128)S(1)} %copy-done.1), kind=kLoop, calls=%fused_computation.6 | loop fusion | flops 3145728 | bytes 8388608 | tf_op jit(solution)/shard_map/stack | solution.py:53
  161.3 0.0 reduce-scatter.3.cloned.1.call-update
  161.3 0.0 reduce-scatter.5.cloned.1.call-start
  161.3 48.1 %reduce-scatter.3.cloned.1.call-done = f32[4,128,512]{2,1,0:T(8,128)} async-done(((f32[4,128,2048]{2,1,0:T(8,128)}), f32[4,128,512]{2,1,0:T(8,128)}) %reduce-scatter.3.cloned.1.call-update) | async-done | bytes 1048592 | tf_op jit(solution)/shard_map/reduce_scatter | solution.py:31
  209.4 0.0 reduce-scatter.5.cloned.1.call-update
  209.5 26.4 %reduce-scatter.5.cloned.1.call-done = f32[4,128,256]{2,1,0:T(8,128)} async-done(((f32[4,128,512]{2,1,0:T(8,128)}), f32[4,128,256]{2,1,0:T(8,128)}) %reduce-scatter.5.cloned.1.call-update) | async-done | bytes 524304 | tf_op jit(solution)/shard_map/reduce_scatter | solution.py:31
  235.9 0.0 copy-done.2
  235.9 1.9 broadcast_multiply_fusion
  (9 shorter events, 0.0 us)
Async XLA Ops:
  6.5 117.7 %all-gather.2.cloned.1.call-start = ((), (), s32[]{:S(2)}) async-start(), calls=%async_computation.3 | async-start | bytes 17825792 | tf_op jit(solution)/shard_map/all_gather | solution.py:41
  26.2 183.2 %reduce-scatter.3.cloned.1.call-start = ((), (), s32[]{:S(2)}) async-start(), calls=%async_computation.4 | async-start | bytes 5242880 | tf_op jit(solution)/shard_map/reduce_scatter | solution.py:31
  124.3 12.6 %slice-start = ((s8[16777216]{0:T(1024)(128)(4,1)}), s8[4194304]{0:T(1024)(128)(4,1)S(1)}, s32[]{:S(2)}) async-start(s8[16777216]{0:T(1024)(128)(4,1)} %bitcast.14), calls=%async_computation.6 | async-start | bytes 8388608
  125.9 10.9 %slice-start.1 = ((s8[16777216]{0:T(1024)(128)(4,1)}), s8[4194304]{0:T(1024)(128)(4,1)S(1)}, s32[]{:S(2)}) async-start(s8[16777216]{0:T(1024)(128)(4,1)} %bitcast.14), calls=%async_computation.7 | async-start | bytes 8388608
  125.9 10.9 %slice-start.2 = ((s8[16777216]{0:T(1024)(128)(4,1)}), s8[4194304]{0:T(1024)(128)(4,1)S(1)}, s32[]{:S(2)}) async-start(s8[16777216]{0:T(1024)(128)(4,1)} %bitcast.14), calls=%async_computation.8 | async-start | bytes 8388608
  125.9 11.0 %slice-start.3 = ((s8[16777216]{0:T(1024)(128)(4,1)}), s8[4194304]{0:T(1024)(128)(4,1)S(1)}, s32[]{:S(2)}) async-start(s8[16777216]{0:T(1024)(128)(4,1)} %bitcast.14), calls=%async_computation.9 | async-start | bytes 8388608
  125.9 15.6 %collective-permute-start = (bf16[16,2048]{1,0:T(8,128)(2,1)}, bf16[16,2048]{1,0:T(8,128)(2,1)S(1)}, u32[]{:S(2)}, u32[]{:S(2)}) collective-permute-start(bf16[16,2048]{1,0:T(8,128)(2,1)} %slice.16), channel_id=1, source_target_pairs={{16,0},{32,16},{48,32},{64,48},{80,64},{96,80},{112,96},{17,1},{33... | collective-permute-start | bytes 196616 | tf_op jit(solution)/shard_map/ppermute | solution.py:26
  141.5 3.7 %copy-start = (bf16[4096,128]{1,0:T(8,128)(2,1)S(1)}, bf16[4096,128]{1,0:T(8,128)(2,1)}, u32[]{:S(2)}) copy-start(bf16[4096,128]{1,0:T(8,128)(2,1)} %subtract_convert_fusion) | copy-start | bytes 3145732
  151.3 6.1 %copy-start.1 = (f32[1,128,2048]{2,1,0:T(8,128)S(1)}, f32[1,128,2048]{2,1,0:T(8,128)}, u32[]{:S(2)}) copy-start(f32[1,128,2048]{2,1,0:T(8,128)} %convolution_bitcast_fusion) | copy-start | bytes 3145732
  151.3 84.5 %copy-start.2 = (f32[4]{0:T(128)S(1)}, f32[4]{0:T(128)}, u32[]{:S(2)}) copy-start(f32[4]{0:T(128)} %constant.13) | copy-start | bytes 52
  161.3 74.6 %reduce-scatter.5.cloned.1.call-start = ((), (), s32[]{:S(2)}) async-start(), calls=%async_computation.5 | async-start | bytes 1572864 | tf_op jit(solution)/shard_map/reduce_scatter | solution.py:31
Sparse Core Ops, SparseCore 0:
  26.3 97.8 all-gather.1
  161.4 47.9 reduce-scatter.2
  211.9 23.8 reduce-scatter.4
where the time goes:
time: 245 us; the launch traced here: 244 us
  waiting for transfers between devices  173 us (71%)
  matrix products  20.5 us (8%)
  blocking collectives  14.8 us (6%)
  between operations  13.2 us (5%)
  local copies, waits for them, and re-layouts  11 us (4%)
  other arithmetic  10.6 us (4%)
    all_gather x1, waiting for transfers between devices, shards(): gathered = lax.all_gather(centered, 'feat', axis=1, tiled=True)  98 us
    reduce_scatter x2, waiting for transfers between devices, summed_rows(): array = lax.psum_scatter(array, axis, scatter_dimension=dim, tiled=True)  74.5 us
    dot_general x4, matrix products, shards(): lax.dot_general(centered, extended[lag:lag + rows], (((0,), (0,)), ((), (...  20.5 us
    all_to_all x1, blocking collectives, copy_for_each(): lax.all_to_all(jnp.broadcast_to(array[None], (length, *array.shape)), axi...  14.8 us
    unnamed x15, local copies, waits for them, and re-layouts  9.39 us
  transfers between devices with their start and end apart: 4, of which 3 were waited for; matrix products, arithmetic and copies ran while one was open for 6% of the time, Pallas kernels for 0%

commit v1 on v0

--- a/solution.py
+++ b/solution.py
@@ -33,12 +33,18 @@
 
 
 def shards(trajectory):
+
+    def step_on_stacks_all(arr_in, axis_k):
+        return jnp.concatenate(
+            lax.all_to_all(jnp.stack(lax.axis_size("feat") * [arr_in]), "feat", 0, 0), axis_k
+        )
+
     rows = trajectory.shape[0]
     frames = rows * lax.axis_size(TM)
     total = over_copies(jnp.sum(trajectory, axis=0), TM)
     mean = total / frames
     centered = (trajectory - mean).astype(jnp.bfloat16)
-    gathered = lax.all_gather(centered, "feat", axis=1, tiled=True)
+    gathered = step_on_stacks_all(centered, 1)
     tail = passed_along(gathered[:HALO], TM, -1)
     extended = jnp.concatenate([gathered, tail], axis=0)
     blocks = [

time: 245 us -> 368 us (1.50)
  blocking collectives: 14.8 us -> 205 us
  waiting for transfers between devices: 173 us -> 74.8 us
  matrix products: 20.5 us -> 54.5 us
    all_to_all x0 -> x1, blocking collectives: none -> 190 us  [step_on_stacks_all(): lax.all_to_all(jnp.stack(lax.axis_size('feat') * [arr_in]), 'feat', 0, 0)]
    all_gather x1 -> x0, waiting for transfers between devices: 98 us -> none  [shards(): gathered = lax.all_gather(centered, 'feat', axis=1, tiled=True)]
    dot_general x4, matrix products: 20.5 us -> 54.5 us  [shards(): lax.dot_general(centered, extended[lag:lag + rows], (((0,), (0,)), ((), (...]
    unnamed x15 -> x6, local copies, waits for them, and re-layouts: 9.39 us -> 5.72 us
  transfers between devices with their start and end apart: 4 -> 3, of which waited for: 3 -> 3; matrix products, arithmetic and copies ran while one was open for 6% -> 3% of each run, Pallas kernels for 0% -> 0%
where the time goes in v1:
time: 368 us; the launch traced here: 367 us
  blocking collectives  205 us (56%)
  waiting for transfers between devices  74.8 us (20%)
  matrix products  54.5 us (15%)
  between operations  13.5 us (4%)
  other arithmetic  9.65 us (3%)
  local copies, waits for them, and re-layouts  8.37 us (2%)
    all_to_all x1, blocking collectives, step_on_stacks_all(): lax.all_to_all(jnp.stack(lax.axis_size('feat') * [arr_in]), 'feat', 0, 0)  190 us
    reduce_scatter x2, waiting for transfers between devices, summed_rows(): array = lax.psum_scatter(array, axis, scatter_dimension=dim, tiled=True)  71.7 us
    dot_general x4, matrix products, shards(): lax.dot_general(centered, extended[lag:lag + rows], (((0,), (0,)), ((), (...  54.5 us
    all_to_all x1, blocking collectives, copy_for_each(): lax.all_to_all(jnp.broadcast_to(array[None], (length, *array.shape)), axi...  14.8 us
  transfers between devices with their start and end apart: 3, of which 3 were waited for; matrix products, arithmetic and copies ran while one was open for 3% of the time, Pallas kernels for 0%

profile of v1, /device:TPU:1, one launch (start us, length us, event | category | flops | bytes accessed | tf_op | source)
XLA Modules:
  0.0 367.3 jit_solution(17904002842989935466)
XLA Ops:
  6.5 0.0 reduce-scatter.3.cloned.1.call-start
  6.5 2.1 reduce_sum.18
  8.7 14.8 %all_to_all.11 = f32[8,1,128]{2,1,0:T(1,128)S(1)} all-to-all(f32[8,1,128]{2,1,0:T(1,128)S(1)} %broadcast_in_dim.2), channel_id=1, replica_groups=mesh['tm_0'=4,'tm_1'=2,'feat'=16] {'tm_0','tm_1'}, dimensions={0} | all-to-all | bytes 8192 | tf_op jit(solution)/shard_map/all_to_all | solution.py:14
  23.5 1.7 subtract_convert_fusion
  25.2 0.5 copy.10
  25.8 2.0 stack.12
  27.7 190.4 %all_to_all.12 = bf16[16,4096,128]{1,2,0:T(8,128)(2,1)S(1)} all-to-all(bf16[16,4096,128]{1,2,0:T(8,128)(2,1)S(1)} %stack.12), channel_id=1, replica_groups=mesh['tm_0'=4,'tm_1'=2,'feat'=16] {'feat'}, dimensions={0} | all-to-all | bytes 33554432 | tf_op jit(solution)/shard_map/all_to_all | solution.py:39
  218.1 0.0 copy-start
  218.1 5.7 %copy-done = bf16[16,4096,128]{1,2,0:T(8,128)(2,1)} copy-done((bf16[16,4096,128]{1,2,0:T(8,128)(2,1)}, bf16[16,4096,128]{1,2,0:T(8,128)(2,1)S(1)}, u32[]{:S(2)}) %copy-start) | copy-done | bytes 16777240
  223.8 0.1 slice.20
  224.0 1.3 collective-permute-start
  225.3 11.5 %convolution_bitcast_fusion = f32[1,128,2048]{2,1,0:T(8,128)S(1)} fusion(bf16[4096,128]{1,0:T(8,128)(2,1)S(1)} %subtract_convert_fusion, bf16[4096,2048]{0,1:T(8,128)(2,1)} %bitcast.19), kind=kOutput, calls=%fused_computation.13 | convolution fusion | flops 2147483648 | bytes 18874368 | tf_op jit(solution)/shard_map/dot_general | solution.py:51
  236.7 0.0 copy-start.1
  236.8 3.0 collective-permute-done
  239.8 15.2 %fusion.14 = f32[1,128,2048]{2,1,0:T(8,128)S(1)} fusion(bf16[4096,128]{1,0:T(8,128)(2,1)S(1)} %subtract_convert_fusion, bf16[16,2048]{0,1:T(8,128)(2,1)} %collective-permute-done, bf16[4096,2048]{0,1:T(8,128)(2,1)} %bitcast.20), kind=kOutput, calls=%fused_computation.15 | convolution fusion | flops 2181038080 | bytes 18939904 | tf_op jit(solution)/shard_map/dot_general | solution.py:51
  255.0 0.0 copy-done.1
  255.1 13.7 %fusion.10 = f32[1,128,2048]{2,1,0:T(8,128)} fusion(bf16[4096,128]{1,0:T(8,128)(2,1)S(1)} %subtract_convert_fusion, bf16[16,2048]{0,1:T(8,128)(2,1)} %collective-permute-done, bf16[4096,2048]{0,1:T(8,128)(2,1)S(1)} %bitcast.21), kind=kOutput, calls=%fused_computation.12 | convolution fusion | flops 2181038080 | bytes 18939904 | tf_op jit(solution)/shard_map/dot_general | solution.py:51
  268.8 0.0 copy-start.2
  268.8 14.0 %fusion.11 = f32[1,128,2048]{2,1,0:T(8,128)} fusion(bf16[4096,128]{1,0:T(8,128)(2,1)S(1)} %subtract_convert_fusion, bf16[16,2048]{0,1:T(8,128)(2,1)} %collective-permute-done, bf16[4096,2048]{0,1:T(8,128)(2,1)S(1)} %bitcast.22), kind=kOutput, calls=%fused_computation.14 | convolution fusion | flops 2181038080 | bytes 18939904 | tf_op jit(solution)/shard_map/dot_general | solution.py:51
  282.8 3.8 %pad_maximum_fusion.2 = f32[4,128,2048]{2,1,0:T(8,128)} fusion(f32[1,128,2048]{2,1,0:T(8,128)} %fusion.10, f32[1,128,2048]{2,1,0:T(8,128)} %fusion.11, f32[1,128,2048]{2,1,0:T(8,128)S(1)} %fusion.14, f32[1,128,2048]{2,1,0:T(8,128)S(1)} %convolution_bitcast_fusion), kind=kLoop, calls=%fused_computation.11 | loop fusion | flops 3145728 | bytes 8388608 | tf_op jit(solution)/shard_map/stack | solution.py:59
  286.6 0.0 reduce-scatter.3.cloned.1.call-update
  286.7 0.0 reduce-scatter.5.cloned.1.call-start
  286.7 45.4 %reduce-scatter.3.cloned.1.call-done = f32[4,128,512]{2,1,0:T(8,128)} async-done(((f32[4,128,2048]{2,1,0:T(8,128)}), f32[4,128,512]{2,1,0:T(8,128)}) %reduce-scatter.3.cloned.1.call-update) | async-done | bytes 1048592 | tf_op jit(solution)/shard_map/reduce_scatter | solution.py:31
  332.1 0.0 reduce-scatter.5.cloned.1.call-update
  332.1 26.4 %reduce-scatter.5.cloned.1.call-done = f32[4,128,256]{2,1,0:T(8,128)} async-done(((f32[4,128,512]{2,1,0:T(8,128)}), f32[4,128,256]{2,1,0:T(8,128)}) %reduce-scatter.5.cloned.1.call-update) | async-done | bytes 524304 | tf_op jit(solution)/shard_map/reduce_scatter | solution.py:31
  358.5 0.0 copy-done.2
  358.5 1.9 broadcast_multiply_fusion
  (3 shorter events, 0.0 us)
Async XLA Ops:
  6.5 325.5 %reduce-scatter.3.cloned.1.call-start = ((), (), s32[]{:S(2)}) async-start(), calls=%async_computation.4 | async-start | bytes 5242880 | tf_op jit(solution)/shard_map/reduce_scatter | solution.py:31
  218.1 5.7 %copy-start = (bf16[16,4096,128]{1,2,0:T(8,128)(2,1)}, bf16[16,4096,128]{1,2,0:T(8,128)(2,1)S(1)}, u32[]{:S(2)}) copy-start(bf16[16,4096,128]{1,2,0:T(8,128)(2,1)S(1)} %all_to_all.12) | copy-start | bytes 50331652
  224.0 15.8 %collective-permute-start = (bf16[16,2048]{0,1:T(8,128)(2,1)S(1)}, bf16[16,2048]{0,1:T(8,128)(2,1)}, u32[]{:S(2)}, u32[]{:S(2)}) collective-permute-start(bf16[16,2048]{0,1:T(8,128)(2,1)S(1)} %bitcast.23), channel_id=1, source_target_pairs={{16,0},{32,16},{48,32},{64,48},{80,64},{96,80},{112,96},{17,1},{33... | collective-permute-start | bytes 196616 | tf_op jit(solution)/shard_map/ppermute | solution.py:26
  236.7 18.3 %copy-start.1 = (bf16[16,4096,128]{1,2,0:T(8,128)(2,1)S(1)}, bf16[16,4096,128]{1,2,0:T(8,128)(2,1)}, u32[]{:S(2)}) copy-start(bf16[16,4096,128]{1,2,0:T(8,128)(2,1)} %copy-done) | copy-start | bytes 50331652
  268.8 89.7 %copy-start.2 = (f32[4]{0:T(128)S(1)}, f32[4]{0:T(128)}, u32[]{:S(2)}) copy-start(f32[4]{0:T(128)} %constant.13) | copy-start | bytes 52
  286.7 71.8 %reduce-scatter.5.cloned.1.call-start = ((), (), s32[]{:S(2)}) async-start(), calls=%async_computation.5 | async-start | bytes 1572864 | tf_op jit(solution)/shard_map/reduce_scatter | solution.py:31
Sparse Core Ops, SparseCore 0:
  286.8 45.2 reduce-scatter.2
  334.5 23.8 reduce-scatter.4
